TPU v7x, 32 devices: a whole 2x2x4 slice. The times are simulated.
32 devices in a mesh: dp: 8 (over z, y), row: 2 (over core), col: 2 (over x).
Axes of the slice: x: 2, y: 2, z: 4, core: 2. Of those that a mesh axis runs over, the one named last changes fastest.
Arguments:
- block_input: bfloat16 [4096, 2560], P(('dp', 'col')), may hold values from -6 to 6
- cotangent: bfloat16 [4096, 2560], P(('dp', 'col'), 'row'), may hold values from -6 to 6
- seq_lengths: int32 [32], replicated, may hold values from 16 to 128, as said below
- seq_owner: int32 [32], replicated, may hold values from 0 to 15, as said below
- norm_gain: bfloat16 [2560], P('row'), may hold values from 0.5 to 1.5
- proj_zx: bfloat16 [2560, 2, 5120], P('row', None, 'col'), may hold values from -0.125 to 0.125
- proj_bc: bfloat16 [2560, 256], P('row'), may hold values from -0.125 to 0.125
- proj_dt: bfloat16 [2560, 80], P('row', 'col'), may hold values from -0.125 to 0.125
- proj_out: bfloat16 [5120, 2560], P('col', 'row'), may hold values from -0.078125 to 0.078125
- inner_kernel: float32 [4, 5120], P(None, 'col'), may hold values from -3 to 3
- inner_offset: float32 [5120], P('col'), may hold values from -1.5 to 1.5
- shared_kernel: float32 [4, 256], replicated, may hold values from -3 to 3
- shared_offset: float32 [256], replicated, may hold values from -1.5 to 1.5
- decay_log: float32 [80], P('col'), may hold values from 0 to 2.77
- step_bias: float32 [80], P('col'), may hold values from -6 to -2
- skip_gain: float32 [80], P('col'), may hold values from 0.5 to 1.5
- output_gain: bfloat16 [5120], P('col'), may hold values from 0.5 to 1.5
Outputs:
- block_output: bfloat16 [4096, 2560], P(('dp', 'col'), 'row')
- input_grad: float32 [4096, 2560], P(('dp', 'col'), 'row')
- grad_norm: float32 [2560], P('row')
- grad_inproj: float32 [2560, 2, 5120], P('row', None, 'col')
- grad_shared: float32 [2560, 256], P('row')
- grad_steps: float32 [2560, 80], P('row', 'col')
- grad_outproj: float32 [5120, 2560], P('col', 'row')
- grad_kernel: float32 [4, 5120], P(None, 'col')
- grad_offset: float32 [5120], P('col')
- grad_skernel: float32 [4, 256], replicated
- grad_soffset: float32 [256], replicated
- grad_decay: float32 [80], P('col')
- grad_stepbias: float32 [80], P('col')
- grad_skip: float32 [80], P('col')
- grad_ogain: float32 [5120], P('col')
Inputs may be any that keep to these rules, and one draw needn't show every extreme that they name: `seq_lengths`: the lengths of the 2 sequences of one bucket sum to at most 256; in every draw some bucket holds 2 sequences of exactly 128 rows, so that its sum is 256. `seq_owner`: every bucket owns exactly 2 sequences.
All inputs are finite; a program needn't handle non-finite values.
Results may differ from a plain program's by a relative error of at most 0.0079.
The roundings to bfloat16 on the way count: a program that leaves them out, or rounds other values in their place, can miss the bound.
Values may be sent and summed in bfloat16 or wider, within the bound.
A program may use at most 256 MiB of HBM per device.

v0:
```python
import jax
import jax.numpy as jnp
from jax import lax
from jax.sharding import PartitionSpec as P

D = 2560
DI = 5120
CAP = 256
EPSILON = 1e-05
PRECISE = lax.Precision.HIGHEST


def layout(seq_lengths, seq_owner, bucket, capacity):
    owned = seq_owner == bucket
    owned_len = jnp.where(owned, seq_lengths, 0)
    order = jnp.arange(seq_lengths.shape[0], dtype=jnp.int32)
    starts = jnp.sum(jnp.where(order[None, :] < order[:, None], owned_len[None, :], 0), axis=1)
    places = jnp.arange(capacity, dtype=jnp.int32)[:, None]
    ends = starts + seq_lengths
    inside = owned[None, :] & (places >= starts[None, :]) & (places < ends[None, :])
    live_rows = jnp.any(inside, axis=1)
    seq_index = jnp.arange(seq_lengths.shape[0], dtype=jnp.int32)
    seq_ids = jnp.sum(jnp.where(inside, seq_index[None, :], 0), axis=1)
    seq_ids = jnp.where(live_rows, seq_ids, -1)
    return (seq_ids, live_rows.astype(jnp.float32))


def convolve(channels, kernel, offset, seq_ids, live_rows):
    tap_count = kernel.shape[0]
    summed_in = offset[None, :] + kernel[tap_count - 1][None, :] * channels
    for lag_steps in range(1, tap_count):
        lagged = jnp.concatenate(
            [jnp.zeros((lag_steps, channels.shape[1]), jnp.float32), channels[:-lag_steps]], axis=0
        )
        prior_ids = jnp.concatenate([jnp.full((lag_steps,), -1, jnp.int32), seq_ids[:-lag_steps]])
        same_seq = jnp.where((prior_ids == seq_ids) & (live_rows > 0), 1.0, 0.0).astype(jnp.float32)
        summed_in = (
            summed_in + kernel[tap_count - 1 - lag_steps][None, :] * lagged * same_seq[:, None]
        )
    return summed_in


def mix_bucket(values, bmat, cmat, sizes, rates, skip_gain, ids, live):
    rows_all, head_count, head_dim = values.shape
    lower = jnp.arange(rows_all)[:, None] >= jnp.arange(rows_all)[None, :]
    cumulated = jnp.dot(lower.astype(jnp.float32), rates, precision=PRECISE)
    pair_live = (ids[:, None] == ids[None, :]) & (live[:, None] > 0) & (live[None, :] > 0) & lower
    scores = jnp.dot(cmat, bmat.T, precision=PRECISE)
    gap = jnp.where(pair_live[:, :, None], cumulated[:, None, :] - cumulated[None, :, :], 0.0)
    weights = (
        jnp.exp(gap) * (pair_live.astype(jnp.float32) * scores)[:, :, None] * sizes[None, :, :]
    )
    within = jnp.einsum("tsh,shp->thp", weights, values, precision=PRECISE)
    mixed_out = (within + skip_gain[None, :, None] * values) * live[:, None, None]
    return mixed_out.reshape(rows_all, head_count * head_dim)


def sum_rows_over_dp(part, shared_cols=0):
    piece = lax.psum_scatter(part.astype(jnp.bfloat16), "dp", scatter_dimension=0, tiled=True)
    if shared_cols:
        own = piece.shape[1] - shared_cols
        tail = lax.psum(piece[:, own:].astype(jnp.float32), "col").astype(jnp.bfloat16)
        piece = jnp.concatenate([piece[:, :own], tail], axis=1)
    return lax.all_gather(piece, "dp", axis=0, tiled=True)


def mixer_local(
    conv_in,
    narrow_in,
    inner_kernel,
    inner_offset,
    shared_kernel,
    shared_offset,
    decay_log,
    step_bias,
    skip_gain,
    seq_ids,
    live_rows,
):
    inner_size = inner_kernel.shape[1]
    state_size = shared_kernel.shape[1] // 2
    head_count = decay_log.shape[0]
    shared_in = narrow_in[:, : 2 * state_size]
    step_raw = narrow_in[:, 2 * state_size :]
    mixed_x = jax.nn.silu(convolve(conv_in, inner_kernel, inner_offset, seq_ids, live_rows))
    mixed_bc = jax.nn.silu(convolve(shared_in, shared_kernel, shared_offset, seq_ids, live_rows))
    step_sizes = jax.nn.softplus(step_raw + step_bias[None, :])
    decay_rate = step_sizes * (-jnp.exp(decay_log))[None, :]
    values = mixed_x.reshape(mixed_x.shape[0], head_count, inner_size // head_count)
    return mix_bucket(
        values,
        mixed_bc[:, :state_size],
        mixed_bc[:, state_size:],
        step_sizes,
        decay_rate,
        skip_gain,
        seq_ids,
        live_rows,
    )


def per_device(
    block_input,
    cotangent,
    seq_lengths,
    seq_owner,
    norm_gain,
    proj_zx,
    proj_bc,
    proj_dt,
    proj_out,
    inner_kernel,
    inner_offset,
    shared_kernel,
    shared_offset,
    decay_log,
    step_bias,
    skip_gain,
    output_gain,
):
    row_count = lax.axis_size("row")
    col_count = lax.axis_size("col")
    row_index = lax.axis_index("row")
    col_index = lax.axis_index("col")
    data_index = lax.axis_index("dp")
    width_part = norm_gain.shape[0]
    inner_size = proj_zx.shape[2]
    state_size = proj_bc.shape[1] // 2
    tap_count = inner_kernel.shape[0]
    capacity = CAP
    bucket = data_index * row_count + row_index
    seq_ids, live_rows = layout(seq_lengths, seq_owner, bucket, capacity)
    rscale = lax.rsqrt(
        jnp.mean(jnp.square(block_input.astype(jnp.float32)), axis=1, keepdims=True) + EPSILON
    )
    own_cols = lax.dynamic_slice_in_dim(block_input, row_index * width_part, width_part, 1).astype(
        jnp.float32
    )
    normalized = own_cols * rscale
    gain_f = norm_gain.astype(jnp.float32)
    normed = (normalized * gain_f[None, :]).astype(jnp.bfloat16)
    normed_all = lax.all_gather(normed, "col", axis=0, tiled=True)
    weight_zx = proj_zx.reshape(width_part, 2 * inner_size)
    weight_narrow = jnp.concatenate([proj_bc, proj_dt], axis=1)
    zx_in = lax.psum_scatter(
        jnp.dot(normed_all, weight_zx, preferred_element_type=jnp.float32),
        "row",
        scatter_dimension=0,
        tiled=True,
    )
    narrow_in = lax.psum_scatter(
        jnp.dot(normed_all, weight_narrow, preferred_element_type=jnp.float32),
        "row",
        scatter_dimension=0,
        tiled=True,
    )
    gate_in = zx_in[:, :inner_size]
    conv_in = zx_in[:, inner_size:]

    def local_piece(*operands):
        return mixer_local(*operands, seq_ids, live_rows)

    ssm_rows, pull_back = jax.vjp(
        local_piece,
        conv_in,
        narrow_in,
        inner_kernel,
        inner_offset,
        shared_kernel,
        shared_offset,
        decay_log,
        step_bias,
        skip_gain,
    )
    gated_rows, gate_back = jax.vjp(
        lambda ssm_value, gate_value: ssm_value * jax.nn.silu(gate_value), ssm_rows, gate_in
    )
    square_sum = lax.psum(jnp.sum(gated_rows * gated_rows, axis=1), "col")
    rnorm = lax.rsqrt(square_sum / DI + EPSILON)[:, None]
    out_gain = output_gain.astype(jnp.float32)
    branch = (gated_rows * rnorm * out_gain[None, :]).astype(jnp.bfloat16)
    branch_all = lax.all_gather(branch, "row", axis=0, tiled=True)
    row_piece = branch_all
    branch_out = lax.psum_scatter(
        jnp.dot(row_piece, proj_out, preferred_element_type=jnp.float32),
        "col",
        scatter_dimension=0,
        tiled=True,
    )
    block_output = (own_cols + branch_out).astype(jnp.bfloat16)
    cot_all = lax.all_gather(cotangent, "col", axis=0, tiled=True)
    row_piece = cot_all
    branch_grad = lax.psum_scatter(
        lax.dot_general(
            row_piece, proj_out, (((1,), (1,)), ((), ())), preferred_element_type=jnp.float32
        ),
        "row",
        scatter_dimension=0,
        tiled=True,
    )
    outproj_part = lax.dot_general(
        branch_all, cot_all, (((0,), (0,)), ((), ())), preferred_element_type=jnp.float32
    )
    outproj_total = sum_rows_over_dp(outproj_part).astype(jnp.float32)
    scaled_grad = branch_grad * out_gain[None, :]
    cross_sum = lax.psum(jnp.sum(scaled_grad * gated_rows, axis=1), "col")
    gated_grad = rnorm * scaled_grad - gated_rows * rnorm**3 * (cross_sum / DI)[:, None]
    ogain_part = jnp.sum(branch_grad * gated_rows * rnorm, axis=0)
    ssm_grad, gate_grad = gate_back(gated_grad)
    gate_all = lax.all_gather(gate_grad.astype(jnp.bfloat16), "row", axis=0, tiled=True)
    gate_total = sum_rows_over_dp(
        lax.dot_general(
            normed_all, gate_all, (((0,), (0,)), ((), ())), preferred_element_type=jnp.float32
        )
    )
    local_grads = pull_back(ssm_grad)
    inner_all = lax.all_gather(local_grads[0].astype(jnp.bfloat16), "row", axis=0, tiled=True)
    narrow_all = lax.all_gather(local_grads[1].astype(jnp.bfloat16), "row", axis=0, tiled=True)
    normed_grad = lax.psum_scatter(
        lax.dot_general(
            jnp.concatenate([gate_all, inner_all], axis=1),
            weight_zx,
            (((1,), (1,)), ((), ())),
            preferred_element_type=jnp.float32,
        )
        + lax.dot_general(
            narrow_all, weight_narrow, (((1,), (1,)), ((), ())), preferred_element_type=jnp.float32
        ),
        "col",
        scatter_dimension=0,
        tiled=True,
    )
    inner_total = sum_rows_over_dp(
        lax.dot_general(
            normed_all, inner_all, (((0,), (0,)), ((), ())), preferred_element_type=jnp.float32
        )
    )
    narrow_part = lax.dot_general(
        normed_all, narrow_all, (((0,), (0,)), ((), ())), preferred_element_type=jnp.float32
    )
    narrow_total = sum_rows_over_dp(
        jnp.concatenate([narrow_part[:, 2 * state_size :], narrow_part[:, : 2 * state_size]], 1),
        2 * state_size,
    ).astype(jnp.float32)
    head_count = decay_log.shape[0]
    steps_total = narrow_total[:, :head_count]
    shared_total = narrow_total[:, head_count:]
    inproj_total = jnp.stack([gate_total, inner_total], axis=1).astype(jnp.float32)
    scaled_in = normed_grad * gain_f[None, :]
    norm_part = jnp.sum(normed_grad * normalized, axis=0)
    row_stat = lax.psum(jnp.sum(scaled_in * normalized, axis=1), "row")
    input_grad = cotangent.astype(jnp.float32) + rscale * (
        scaled_in - normalized * (row_stat / D)[:, None]
    )
    row_hot = (jnp.arange(row_count) == row_index).astype(jnp.float32)
    col_hot = (jnp.arange(col_count) == col_index).astype(jnp.float32)
    gain_slot = row_hot[:, None] * norm_part[None, :]
    head_stack = jnp.stack([local_grads[6], local_grads[7], local_grads[8]], axis=0)
    head_slot = col_hot[None, :, None] * head_stack[:, None, :]
    chan_stack = jnp.concatenate(
        [local_grads[2], local_grads[3][None, :], ogain_part[None, :]], axis=0
    )
    chan_slot = col_hot[None, :, None] * chan_stack[:, None, :]
    shared_stack = jnp.concatenate([local_grads[4], local_grads[5][None, :]], axis=0)
    summed = lax.psum((gain_slot, head_slot, chan_slot, shared_stack), ("dp", "row", "col"))
    gain_total = lax.dynamic_index_in_dim(summed[0], row_index, 0, keepdims=False)
    head_total = lax.dynamic_index_in_dim(summed[1], col_index, 1, keepdims=False)
    chan_total = lax.dynamic_index_in_dim(summed[2], col_index, 1, keepdims=False)
    stack_total = summed[3]
    return (
        block_output,
        input_grad,
        gain_total,
        inproj_total,
        shared_total,
        steps_total,
        outproj_total,
        chan_total[:tap_count],
        chan_total[tap_count],
        stack_total[:tap_count],
        stack_total[tap_count],
        head_total[0],
        head_total[1],
        head_total[2],
        chan_total[tap_count + 1],
    )


def solution(mesh):
    return jax.shard_map(
        per_device,
        mesh=mesh,
        in_specs=(
            P(("dp", "col"), None),
            P(("dp", "col"), "row"),
            P(),
            P(),
            P("row"),
            P("row", None, "col"),
            P("row", None),
            P("row", "col"),
            P("col", "row"),
            P(None, "col"),
            P("col"),
            P(),
            P(),
            P("col"),
            P("col"),
            P("col"),
            P("col"),
        ),
        out_specs=(
            P(("dp", "col"), "row"),
            P(("dp", "col"), "row"),
            P("row"),
            P("row", None, "col"),
            P("row", None),
            P("row", "col"),
            P("col", "row"),
            P(None, "col"),
            P("col"),
            P(),
            P(),
            P("col"),
            P("col"),
            P("col"),
            P("col"),
        ),
        check_vma=False,
    )
```

profile of v0, /device:TPU:0, one launch (start us, length us, event | category | flops | bytes accessed | tf_op | source)
XLA Modules:
  0.0 1226.2 jit_solution(14746132511163028913)
XLA Ops:
  12.6 12.3 %copy.74 = bf16[160,8,2,2560]{3,1,2,0:T(8,128)(2,1)} copy(bf16[160,8,2,2560]{3,2,1,0:T(2,128)(2,1)} %bitcast.83) | data formatting | bytes 26214400
  25.1 13.7 %all-gather.9.cloned.1.call-done = bf16[512,1280]{1,0:T(8,128)(2,1)} async-done(((bf16[256,1280]{1,0:T(8,128)(2,1)}), bf16[512,1280]{1,0:T(8,128)(2,1)}) %all-gather.9.cloned.1.call-update) | async-done | bytes 1310736 | tf_op jit(solution)/shard_map/all_gather | solution.py:142
  41.8 12.3 %fusion.106 = f32[512,5120]{1,0:T(8,128)} fusion(bf16[512,1280]{1,0:T(8,128)(2,1)S(1)} %copy-done.17, bf16[1280,5120]{1,0:T(8,128)(2,1)} %bitcast.84), kind=kOutput, calls=%fused_computation.194 | convolution fusion | flops 6710886400 | bytes 24903680 | tf_op jit(solution)/shard_map/dot_general | solution.py:146
  54.2 10.5 all-gather.13.cloned.1.call-done
  64.7 9.2 fusion.108
  83.8 14.8 %reduce-scatter.12.cloned.1.call-done = f32[256,5120]{1,0:T(8,128)} async-done(((f32[512,5120]{1,0:T(8,128)}), f32[256,5120]{1,0:T(8,128)}) %reduce-scatter.12.cloned.1.call-update) | async-done | bytes 5242896 | tf_op jit(solution)/shard_map/reduce_scatter | solution.py:145
  110.1 15.6 %fusion.33 = f32[256,40,64]{0,2,1:T(8,128)} fusion(f32[256,40,64]{0,2,1:T(8,128)} %bitcast.88, f32[256,40]{0,1:T(8,128)S(1)} %compare_select_fusion.2, f32[256,256]{1,0:T(8,128)} %convolution_select_fusion, f32[256,40]{0,1:T(8,128)S(1)} %fusion.64, pred[256,256]{1,0:T(8,128)(4,1)S(1)} %fusion.65, f32[256]{0:T(256)S(1)} %get-tuple-element.145, ...), kind=kOutput, calls=%fused_computation.49 | convolution fusion | flops 2025717760 | bytes 5653664 | tf_op jit(solution)/shard_map/jvp(tsh,shp->thp)/dot_general | solution.py:53
  154.2 11.6 bitcast_add_fusion
  182.7 18.6 %fusion.8 = (f32[256,40]{0,1:T(8,128)}, f32[256,40]{0,1:T(8,128)}, f32[256,40]{0,1:T(8,128)}, f32[256,256]{1,0:T(8,128)S(1)}) fusion(f32[256,40]{0,1:T(8,128)} %copy-done.31, f32[256,256]{1,0:T(8,128)} %convolution_select_fusion, f32[256,40]{0,1:T(8,128)} %copy-done.66, pred[256,256]{1,0:T(8,128)(4,1)S(1)} %fusion.65, f32[256,40,64]{0,2,1:T(8,128)S(1)} %bitcast.89, ...), kind=kOutput, calls=%fused_computation.15 | convolution fusion | flops 2047903744 | bytes 6038528 | tf_op jit(solution)/shard_map/transpose(jvp(tsh,shp->thp))/dot_general | solution.py:53
  236.7 55.0 %reduce-scatter.28.cloned.1.call-done = bf16[160,296]{1,0:T(8,128)(2,1)} async-done(((bf16[1280,296]{1,0:T(8,128)(2,1)}), bf16[160,296]{1,0:T(8,128)(2,1)}) %reduce-scatter.28.cloned.1.call-update) | async-done | bytes 94736
  293.5 13.9 %fusion.9 = f32[512,1280]{1,0:T(8,128)} fusion(bf16[1280,5120]{1,0:T(8,128)(2,1)} %bitcast.85, bf16[512,2560]{1,0:T(8,128)(2,1)} %all-gather.17.cloned.1.call-done, bf16[512,2560]{1,0:T(8,128)(2,1)} %all-gather.15.cloned.1.call-done), kind=kOutput, calls=%fused_computation.16 | convolution fusion | flops 6721372160 | bytes 20971520 | tf_op jit(solution)/shard_map/dot_general | solution.py:220
  321.2 95.2 %reduce-scatter.24.cloned.1.call-done = bf16[160,2560]{1,0:T(8,128)(2,1)} async-done(((bf16[1280,2560]{1,0:T(8,128)(2,1)}), bf16[160,2560]{1,0:T(8,128)(2,1)}) %reduce-scatter.24.cloned.1.call-update) | async-done | bytes 819216 | tf_op jit(solution)/shard_map/reduce_scatter | solution.py:59
  416.4 124.8 %reduce-scatter.22.cloned.1.call-done = bf16[160,2560]{1,0:T(8,128)(2,1)} async-done(((bf16[1280,2560]{1,0:T(8,128)(2,1)}), bf16[160,2560]{1,0:T(8,128)(2,1)}) %reduce-scatter.22.cloned.1.call-update) | async-done | bytes 819216 | tf_op jit(solution)/shard_map/reduce_scatter | solution.py:59
  541.3 124.2 %reduce-scatter.26.cloned.1.call-done = bf16[320,1280]{1,0:T(8,128)(2,1)} async-done(((bf16[2560,1280]{1,0:T(8,128)(2,1)}), bf16[320,1280]{1,0:T(8,128)(2,1)}) %reduce-scatter.26.cloned.1.call-update) | async-done | bytes 819216 | tf_op jit(solution)/shard_map/reduce_scatter | solution.py:59
  665.9 127.6 %all-reduce.32.cloned.1.call-done = f32[6,2,2560]{2,0,1:T(8,128)} async-done(((f32[6,2,2560]{2,0,1:T(8,128)}), f32[6,2,2560]{2,0,1:T(8,128)}) %all-reduce.32.cloned.1.call-update) | async-done | bytes 122896 | tf_op jit(solution)/shard_map/psum | solution.py:265
  796.7 23.0 %all-reduce.30.cloned.1.call-done = bf16[160,256]{0,1:T(8,128)(2,1)} async-done(((bf16[160,256]{0,1:T(8,128)(2,1)}), bf16[160,256]{0,1:T(8,128)(2,1)}) %all-reduce.30.cloned.1.call-update) | async-done | bytes 81936 | tf_op jit(solution)/shard_map/psum | solution.py:62
  820.8 33.0 %all_gather.38 = bf16[1280,296]{1,0:T(8,128)(2,1)S(1)} all-gather(bf16[160,296]{1,0:T(8,128)(2,1)S(1)} %copy.67), channel_id=1, replica_groups=mesh['dp'=8,'row'=2,'col'=2] {'dp'}, dimensions={0}, use_global_device_ids=true | all-gather | bytes 852480 | tf_op jit(solution)/shard_map/all_gather | solution.py:64
  862.1 40.3 %all-reduce.26 = (f32[2,1280]{1,0:T(2,128)S(1)}, f32[5,256]{1,0:T(8,128)S(1)}, f32[3,2,40]{2,1,0:T(2,128)S(1)}) all-reduce(f32[2,1280]{1,0:T(2,128)S(1)} %broadcast_multiply_fusion.7, f32[5,256]{1,0:T(8,128)S(1)} %pad_maximum_fusion.6, ...), channel_id=1, replica_groups=mesh['dp'=8,'row'=2,'col'=2] {'dp','row','col'}, use_global_device_ids=true, to_apply=%region_20.21 | all-reduce | flops 4080 | bytes 32640 | tf_op jit(solution)/shard_map/psum | solution.py:265
  910.2 94.8 %all-gather.21.cloned.1.call-done = bf16[1280,2560]{1,0:T(8,128)(2,1)} async-done(((bf16[160,2560]{1,0:T(8,128)(2,1)}), bf16[1280,2560]{1,0:T(8,128)(2,1)}) %all-gather.21.cloned.1.call-update) | async-done | bytes 6553616 | tf_op jit(solution)/shard_map/all_gather | solution.py:64
  1005.0 102.7 %all-gather.19.cloned.1.call-done = bf16[1280,2560]{1,0:T(8,128)(2,1)} async-done(((bf16[160,2560]{1,0:T(8,128)(2,1)}), bf16[1280,2560]{1,0:T(8,128)(2,1)}) %all-gather.19.cloned.1.call-update) | async-done | bytes 6553616 | tf_op jit(solution)/shard_map/all_gather | solution.py:64
  1107.7 14.4 %maximum_convert_fusion = f32[1280,2,2560]{2,0,1:T(8,128)} fusion(bf16[1280,1,2560]{2,0,1:T(8,128)(2,1)} %bitcast.86, bf16[1280,1,2560]{2,0,1:T(8,128)(2,1)} %bitcast.87), kind=kLoop, calls=%fused_computation | loop fusion | flops 13107200 | bytes 39321600 | tf_op jit(solution)/shard_map/convert_element_type | solution.py:248
  1122.1 43.6 %copy.68 = f32[1280,2,2560]{2,1,0:T(2,128)} copy(f32[1280,2,2560]{2,0,1:T(8,128)} %maximum_convert_fusion) | data formatting | bytes 52428800
  1165.7 44.9 %all-gather.23.cloned.1.call-done = bf16[2560,1280]{1,0:T(8,128)(2,1)} async-done(((bf16[320,1280]{1,0:T(8,128)(2,1)}), bf16[2560,1280]{1,0:T(8,128)(2,1)}) %all-gather.23.cloned.1.call-update) | async-done | bytes 6553616 | tf_op jit(solution)/shard_map/all_gather | solution.py:64
  1210.6 8.8 convert_element_type.112
  (291 shorter events, 146.2 us)
Async XLA Ops:
  7.2 31.7 %all-gather.9.cloned.1.call-start = ((), (), s32[]{:S(2)}) async-start(), calls=%async_computation.9 | async-start | bytes 1966080 | tf_op jit(solution)/shard_map/all_gather | solution.py:142
  11.8 52.9 %all-gather.13.cloned.1.call-start = ((), (), s32[]{:S(2)}) async-start(), calls=%async_computation.14 | async-start | bytes 1966080 | tf_op jit(solution)/shard_map/all_gather | solution.py:191
  12.5 63.1 %reduce-scatter.14.cloned.1.call-start = ((), (), s32[]{:S(2)}) async-start(), calls=%async_computation.11 | async-start | bytes 909312 | tf_op jit(solution)/shard_map/reduce_scatter | solution.py:151
  41.8 56.8 %reduce-scatter.12.cloned.1.call-start = ((), (), s32[]{:S(2)}) async-start(), calls=%async_computation.10 | async-start | bytes 15728640 | tf_op jit(solution)/shard_map/reduce_scatter | solution.py:145
  54.2 82.6 %reduce-scatter.18.cloned.1.call-start = ((), (), s32[]{:S(2)}) async-start(), calls=%async_computation.15 | async-start | bytes 7864320 | tf_op jit(solution)/shard_map/reduce_scatter | solution.py:193
  74.0 136.6 %all-gather.17.cloned.1.call-start = ((), (), s32[]{:S(2)}) async-start(), calls=%async_computation.17 | async-start | bytes 3932160 | tf_op jit(solution)/shard_map/all_gather | solution.py:217
  75.2 94.0 %copy-start.37 = (f32[256]{0:T(256)}, f32[256]{0:T(256)S(1)}, u32[]{:S(2)}) copy-start(f32[256]{0:T(256)S(1)} %get-tuple-element.142) | copy-start | bytes 3076
  75.2 98.1 %copy-start.33 = (f32[256]{0:T(256)}, f32[256]{0:T(256)S(1)}, u32[]{:S(2)}) copy-start(f32[256]{0:T(256)S(1)} %get-tuple-element.140) | copy-start | bytes 3076
  75.2 98.1 %copy-start.35 = (f32[256]{0:T(256)}, f32[256]{0:T(256)S(1)}, u32[]{:S(2)}) copy-start(f32[256]{0:T(256)S(1)} %get-tuple-element.141) | copy-start | bytes 3076
  180.9 37.0 %all-gather.15.cloned.1.call-start = ((), (), s32[]{:S(2)}) async-start(), calls=%async_computation.16 | async-start | bytes 3932160 | tf_op jit(solution)/shard_map/all_gather | solution.py:210
  181.7 44.2 %all-gather.11.cloned.1.call-start = ((), (), s32[]{:S(2)}) async-start(), calls=%async_computation.12 | async-start | bytes 3932160 | tf_op jit(solution)/shard_map/all_gather | solution.py:182
  202.0 89.6 %reduce-scatter.28.cloned.1.call-start = ((), (), s32[]{:S(2)}) async-start(), calls=%async_computation.27 | async-start | bytes 1105920
  210.5 205.8 %reduce-scatter.24.cloned.1.call-start = ((), (), s32[]{:S(2)}) async-start(), calls=%async_computation.21 | async-start | bytes 7372800 | tf_op jit(solution)/shard_map/reduce_scatter | solution.py:59
  217.9 323.3 %reduce-scatter.22.cloned.1.call-start = ((), (), s32[]{:S(2)}) async-start(), calls=%async_computation.19 | async-start | bytes 7372800 | tf_op jit(solution)/shard_map/reduce_scatter | solution.py:59
  225.6 439.9 %reduce-scatter.26.cloned.1.call-start = ((), (), s32[]{:S(2)}) async-start(), calls=%async_computation.24 | async-start | bytes 7372800 | tf_op jit(solution)/shard_map/reduce_scatter | solution.py:59
  235.0 558.5 %all-reduce.32.cloned.1.call-start = ((), (), s32[]{:S(2)}) async-start(), calls=%async_computation.26 | async-start | bytes 327680 | tf_op jit(solution)/shard_map/psum | solution.py:265
  236.6 583.1 %all-reduce.30.cloned.1.call-start = ((), (), s32[]{:S(2)}) async-start(), calls=%async_computation.23 | async-start | bytes 262144 | tf_op jit(solution)/shard_map/psum | solution.py:62
  293.4 566.7 %reduce-scatter.20.cloned.1.call-start = ((), (), s32[]{:S(2)}) async-start(), calls=%async_computation.18 | async-start | bytes 3932160 | tf_op jit(solution)/shard_map/reduce_scatter | solution.py:219
  311.5 595.6 %reduce-scatter.16.cloned.1.call-start = ((), (), s32[]{:S(2)}) async-start(), calls=%async_computation.13 | async-start | bytes 3932160 | tf_op jit(solution)/shard_map/reduce_scatter | solution.py:184
  321.1 344.6 %copy-start.63 = (f32[40]{0:T(128)S(1)}, f32[40]{0:T(128)}, u32[]{:S(2)}) copy-start(f32[40]{0:T(128)} %param.30) | copy-start | bytes 484
  321.1 475.5 %slice-start.2 = ((bf16[160,296]{1,0:T(8,128)(2,1)}), bf16[160,40]{1,0:T(8,128)(2,1)S(1)}, s32[]{:S(2)}) async-start(bf16[160,296]{1,0:T(8,128)(2,1)} %reduce-scatter.28.cloned.1.call-done), calls=%async_computation.30 | async-start | bytes 81920 | tf_op jit(solution)/shard_map/slice | solution.py:63
  321.2 683.9 %all-gather.21.cloned.1.call-start = ((), (), s32[]{:S(2)}) async-start(), calls=%async_computation.22 | async-start | bytes 7372800 | tf_op jit(solution)/shard_map/all_gather | solution.py:64
  416.4 691.4 %all-gather.19.cloned.1.call-start = ((), (), s32[]{:S(2)}) async-start(), calls=%async_computation.20 | async-start | bytes 7372800 | tf_op jit(solution)/shard_map/all_gather | solution.py:64
  541.2 669.3 %all-gather.23.cloned.1.call-start = ((), (), s32[]{:S(2)}) async-start(), calls=%async_computation.25 | async-start | bytes 7372800 | tf_op jit(solution)/shard_map/all_gather | solution.py:64
  (65 other events, 773.5 us)
Sparse Core Ops, SparseCore 0:
  11.9 26.9 all-gather.8
  40.4 24.2 all-gather.12
  67.6 8.0 reduce-scatter.13
  78.4 20.1 reduce-scatter.11
  100.8 14.4 reduce-scatter.17
  181.1 12.5 all-gather.16
  195.9 12.6 all-gather.14
  210.8 12.5 all-gather.10
  227.1 64.4 reduce-scatter.27
  295.7 120.6 reduce-scatter.23
  420.4 120.7 reduce-scatter.21
  544.7 120.7 reduce-scatter.25
  672.5 120.9 all-reduce.31
  796.3 23.4 all-reduce.29
  822.5 37.5 reduce-scatter.19
  862.2 38.2 reduce-scatter.15
  902.8 102.1 all-gather.20
  1007.3 100.3 all-gather.18
  1110.1 100.3 all-gather.22
where the time goes:
time: 1230 us
  waiting for transfers between devices  837 us (68%)
  matrix products  124 us (10%)
  local copies, waits for them, and re-layouts  92.5 us (8%)
  blocking collectives  87.9 us (7%)
  other arithmetic  67.7 us (6%)
  between operations  15.3 us (1%)
    reduce_scatter x3, waiting for transfers between devices, sum_rows_over_dp(): lax.psum_scatter(part.astype(jnp.bfloat16), 'dp', scatter_dimension=0, ti...  344 us
    all_gather x3, waiting for transfers between devices, sum_rows_over_dp(): return lax.all_gather(piece, 'dp', axis=0, tiled=True)  242 us
    psum x1, waiting for transfers between devices, per_device(): lax.psum((gain_slot, head_slot, chan_slot, shared_stack), ('dp', 'row', '...  128 us
    unnamed x145, local copies, waits for them, and re-layouts  68.9 us
    unnamed x20, waiting for transfers between devices  56.6 us
    dot_general x3, matrix products, mix_bucket(): within = jnp.einsum('tsh,shp->thp', weights, values, precision=PRECISE)  45.7 us
    psum x1, blocking collectives, per_device(): lax.psum((gain_slot, head_slot, chan_slot, shared_stack), ('dp', 'row', '...  40.3 us
    all_gather x1, blocking collectives, sum_rows_over_dp(): return lax.all_gather(piece, 'dp', axis=0, tiled=True)  33 us
  transfers between devices with their start and end apart: 19, of which 14 were waited for; matrix products, arithmetic and copies ran while one was open for 18% of the time, Pallas kernels for 0%

commit v1 on v0

--- a/solution.py
+++ b/solution.py
@@ -8,6 +8,18 @@
 CAP = 256
 EPSILON = 1e-05
 PRECISE = lax.Precision.HIGHEST
+
+
+def doubled_up(shard, axis, dim):
+    ways, here, lap = (lax.axis_size(axis), lax.axis_index(axis), shard.shape[dim])
+    line, have = (shard, 1)
+    while have < ways:
+        line = jnp.concatenate(
+            [line, lax.ppermute(line, axis, [(d, (d - have) % ways) for d in range(ways)])],
+            axis=dim,
+        )
+        have = 2 * have
+    return jnp.roll(line, here * lap, axis=dim)
 
 
 def layout(seq_lengths, seq_owner, bucket, capacity):
@@ -61,7 +73,7 @@
         own = piece.shape[1] - shared_cols
         tail = lax.psum(piece[:, own:].astype(jnp.float32), "col").astype(jnp.bfloat16)
         piece = jnp.concatenate([piece[:, :own], tail], axis=1)
-    return lax.all_gather(piece, "dp", axis=0, tiled=True)
+    return doubled_up(piece, "dp", 0)
 
 
 def mixer_local(

time: 1230 us -> 1550 us (1.26)
  starting transfers between devices: 1.53 us -> 197 us
  other arithmetic: 67.7 us -> 147 us
  waiting for transfers between devices: 837 us -> 881 us
    ppermute x0 -> x12, waiting for transfers between devices: none -> 278 us  [doubled_up(): lax.ppermute(line, axis, [(d, (d - have) % ways) for d in range(ways)])]
    all_gather x3 -> x0, waiting for transfers between devices: 242 us -> none  [sum_rows_over_dp(): return lax.all_gather(piece, 'dp', axis=0, tiled=True)]
    ppermute x0 -> x12, starting transfers between devices: none -> 196 us  [doubled_up(): lax.ppermute(line, axis, [(d, (d - have) % ways) for d in range(ways)])]
    another operation x0 -> x2, other arithmetic: none -> 60 us  [per_device(): jnp.stack([gate_total, inner_total], axis=1).astype(jnp.float32)]
    reduce_scatter x3, waiting for transfers between devices: 344 us -> 288 us  [sum_rows_over_dp(): lax.psum_scatter(part.astype(jnp.bfloat16), 'dp', scatter_dimension=0, ti...]
    all_gather x1 -> x0, blocking collectives: 33 us -> none  [sum_rows_over_dp(): return lax.all_gather(piece, 'dp', axis=0, tiled=True)]
    reduce_scatter x1, waiting for transfers between devices: 4.07 us -> 34.1 us  [per_device(): lax.psum_scatter(lax.dot_general(jnp.concatenate([gate_all, inner_all], a...]
    psum x1, waiting for transfers between devices: 128 us -> 149 us  [per_device(): lax.psum((gain_slot, head_slot, chan_slot, shared_stack), ('dp', 'row', '...]
  transfers between devices with their start and end apart: 19 -> 28, of which waited for: 14 -> 17; matrix products, arithmetic and copies ran while one was open for 18% -> 20% of each run, Pallas kernels for 0% -> 0%
where the time goes in v1:
time: 1550 us; the launch traced here: 1540 us
  waiting for transfers between devices  881 us (57%)
  starting transfers between devices  197 us (13%)
  other arithmetic  147 us (9%)
  matrix products  120 us (8%)
  local copies, waits for them, and re-layouts  107 us (7%)
  blocking collectives  75.6 us (5%)
    reduce_scatter x3, waiting for transfers between devices, sum_rows_over_dp(): lax.psum_scatter(part.astype(jnp.bfloat16), 'dp', scatter_dimension=0, ti...  288 us
    ppermute x12, waiting for transfers between devices, doubled_up(): lax.ppermute(line, axis, [(d, (d - have) % ways) for d in range(ways)])  278 us
    ppermute x12, starting transfers between devices, doubled_up(): lax.ppermute(line, axis, [(d, (d - have) % ways) for d in range(ways)])  196 us
    psum x1, waiting for transfers between devices, per_device(): lax.psum((gain_slot, head_slot, chan_slot, shared_stack), ('dp', 'row', '...  149 us
    unnamed x190, local copies, waits for them, and re-layouts  80.4 us
    psum x1, blocking collectives, per_device(): lax.psum((gain_slot, head_slot, chan_slot, shared_stack), ('dp', 'row', '...  61.1 us
    another operation x2, other arithmetic, per_device(): jnp.stack([gate_total, inner_total], axis=1).astype(jnp.float32)  60 us
    unnamed x17, waiting for transfers between devices  48.5 us
  transfers between devices with their start and end apart: 28, of which 17 were waited for; matrix products, arithmetic and copies ran while one was open for 20% of the time, Pallas kernels for 0%

profile of v1, /device:TPU:0, one launch (start us, length us, event | category | flops | bytes accessed | tf_op | source)
XLA Modules:
  0.0 1543.0 jit_solution(664375025401396336)
XLA Ops:
  12.9 12.3 copy.71
  25.2 13.7 all-gather.6.cloned.1.call-done
  41.8 12.3 fusion.123
  84.7 13.9 reduce-scatter.12.cloned.1.call-done
  110.3 15.8 %fusion.49 = f32[256,40,64]{0,2,1:T(8,128)} fusion(f32[256,40,64]{0,2,1:T(8,128)} %bitcast.90, f32[256,40]{0,1:T(8,128)} %copy-done.38, f32[256,256]{1,0:T(8,128)} %convolution_select_fusion, f32[256,40]{0,1:T(8,128)} %fusion.80, pred[256,256]{1,0:T(8,128)(4,1)S(1)} %fusion.81, f32[256]{0:T(256)S(1)} %copy-done.63, f32[40]{0:T(128)S(1)} %copy-done.80), kind=kOutput, calls=%fused_computation.85 | convolution fusion | flops 2025717760 | bytes 5653664 | tf_op jit(solution)/shard_map/jvp(tsh,shp->thp)/dot_general | solution.py:65
  155.9 17.5 %fusion.24 = (f32[256,40]{0,1:T(8,128)S(1)}, f32[256,40]{0,1:T(8,128)S(1)}, f32[256,40]{0,1:T(8,128)S(1)}, f32[256,256]{1,0:T(8,128)S(1)}) fusion(f32[256,40]{0,1:T(8,128)} %copy-done.38, f32[256,256]{1,0:T(8,128)} %convolution_select_fusion, f32[256,40]{0,1:T(8,128)} %fusion.80, pred[256,256]{1,0:T(8,128)(4,1)S(1)} %fusion.81, ...), kind=kOutput, calls=%fused_computation.48 | convolution fusion | flops 2047903744 | bytes 6038528 | tf_op jit(solution)/shard_map/transpose(jvp(tsh,shp->thp))/dot_general | solution.py:65
  182.0 11.5 bitcast_add_fusion
  228.2 46.9 %reduce-scatter.28.cloned.1.call-done = bf16[160,296]{1,0:T(8,128)(2,1)} async-done(((bf16[1280,296]{1,0:T(8,128)(2,1)}), bf16[160,296]{1,0:T(8,128)(2,1)}) %reduce-scatter.28.cloned.1.call-update) | async-done | bytes 94736
  287.0 12.7 fusion.25
  331.2 97.4 %reduce-scatter.22.cloned.1.call-done = bf16[160,2560]{1,0:T(8,128)(2,1)} async-done(((bf16[1280,2560]{1,0:T(8,128)(2,1)}), bf16[160,2560]{1,0:T(8,128)(2,1)}) %reduce-scatter.22.cloned.1.call-update) | async-done | bytes 819216 | tf_op jit(solution)/shard_map/reduce_scatter | solution.py:71
  431.2 20.9 %all-reduce.30.cloned.1.call-done = bf16[160,256]{0,1:T(8,128)(2,1)} async-done(((bf16[160,256]{0,1:T(8,128)(2,1)}), bf16[160,256]{0,1:T(8,128)(2,1)}) %all-reduce.30.cloned.1.call-update) | async-done | bytes 81936 | tf_op jit(solution)/shard_map/psum | solution.py:74
  470.3 149.3 %all-reduce.32.cloned.1.call-done = f32[6,2,2560]{2,0,1:T(8,128)} async-done(((f32[6,2,2560]{2,0,1:T(8,128)}), f32[6,2,2560]{2,0,1:T(8,128)}) %all-reduce.32.cloned.1.call-update) | async-done | bytes 122896 | tf_op jit(solution)/shard_map/psum | solution.py:277
  627.4 34.1 %reduce-scatter.20.cloned.1.call-done = f32[256,1280]{1,0:T(8,128)} async-done(((f32[512,1280]{1,0:T(8,128)}), f32[256,1280]{1,0:T(8,128)}) %reduce-scatter.20.cloned.1.call-update) | async-done | bytes 1310736 | tf_op jit(solution)/shard_map/reduce_scatter | solution.py:231
  663.3 123.4 %reduce-scatter.26.cloned.1.call-done = bf16[320,1280]{1,0:T(8,128)(2,1)} async-done(((bf16[2560,1280]{1,0:T(8,128)(2,1)}), bf16[320,1280]{1,0:T(8,128)(2,1)}) %reduce-scatter.26.cloned.1.call-update) | async-done | bytes 819216 | tf_op jit(solution)/shard_map/reduce_scatter | solution.py:71
  789.1 61.1 %all-reduce.26 = (f32[2,1280]{1,0:T(2,128)S(1)}, f32[5,256]{1,0:T(8,128)S(1)}, f32[3,2,40]{2,1,0:T(2,128)S(1)}) all-reduce(f32[2,1280]{1,0:T(2,128)S(1)} %broadcast_multiply_fusion.7, f32[5,256]{1,0:T(8,128)S(1)} %pad_maximum_fusion.14, ...), channel_id=1, replica_groups=mesh['dp'=8,'row'=2,'col'=2] {'dp','row','col'}, use_global_device_ids=true, to_apply=%region_20.21 | all-reduce | flops 4080 | bytes 32640 | tf_op jit(solution)/shard_map/psum | solution.py:277
  854.5 67.4 %reduce-scatter.24.cloned.1.call-done = bf16[160,2560]{1,0:T(8,128)(2,1)} async-done(((bf16[1280,2560]{1,0:T(8,128)(2,1)}), bf16[160,2560]{1,0:T(8,128)(2,1)}) %reduce-scatter.24.cloned.1.call-update) | async-done | bytes 819216 | tf_op jit(solution)/shard_map/reduce_scatter | solution.py:71
  946.2 14.5 reduce-scatter.16.cloned.1.call-done
  966.4 82.1 %collective-permute-done.10 = bf16[640,1280]{1,0:T(8,128)(2,1)S(1)} collective-permute-done((bf16[640,1280]{1,0:T(8,128)(2,1)}, bf16[640,1280]{1,0:T(8,128)(2,1)S(1)}, u32[]{:S(2)}, u32[]{:S(2)}) %collective-permute-start.10) | collective-permute-done | bytes 1638432 | tf_op jit(solution)/shard_map/ppermute | solution.py:18
  1048.9 70.9 %collective-permute-start.11 = (bf16[1280,1280]{1,0:T(8,128)(2,1)S(1)}, bf16[1280,1280]{1,0:T(8,128)(2,1)S(1)}, u32[]{:S(2)}, u32[]{:S(2)}) collective-permute-start(bf16[1280,1280]{1,0:T(8,128)(2,1)S(1)} %pad_maximum_fusion.2), channel_id=1, source_target_pairs={{0,16},{4,20},{8,24},{12,28},{16,0},{20,4},{24,8},{28,12},{1,17},{... | collective-permute-start | bytes 9830408 | tf_op jit(solution)/shard_map/ppermute | solution.py:18
  1121.4 105.0 %collective-permute-start.5 = (bf16[640,2560]{1,0:T(8,128)(2,1)S(1)}, bf16[640,2560]{1,0:T(8,128)(2,1)S(1)}, u32[]{:S(2)}, u32[]{:S(2)}) collective-permute-start(bf16[640,2560]{1,0:T(8,128)(2,1)S(1)} %pad_maximum_fusion.1), channel_id=1, source_target_pairs={{0,16},{4,20},{8,24},{12,28},{16,0},{20,4},{24,8},{28,12},{1,17},{... | collective-permute-start | bytes 9830408 | tf_op jit(solution)/shard_map/ppermute | solution.py:18
  1227.7 26.8 %fusion.19 = bf16[1280,1,2560]{2,0,1:T(8,128)(2,1)S(1)} fusion(s32[]{:T(128)S(6)} %select_n.129, bf16[160,2560]{1,0:T(8,128)(2,1)S(1)} %copy-done.12, bf16[160,2560]{1,0:T(8,128)(2,1)S(1)} %copy-done.16, bf16[320,2560]{1,0:T(8,128)(2,1)} %collective-permute-done.1, bf16[640,2560]{1,0:T(8,128)(2,1)} %collective-permute-done.2), kind=kLoop, calls=%fused_computation.42 | loop fusion | flops 52428800 | bytes 13107204 | tf_op jit(solution)/shard_map/stack | solution.py:260
  1254.5 179.9 %collective-permute-done.5 = bf16[640,2560]{1,0:T(8,128)(2,1)S(1)} collective-permute-done((bf16[640,2560]{1,0:T(8,128)(2,1)S(1)}, bf16[640,2560]{1,0:T(8,128)(2,1)S(1)}, u32[]{:S(2)}, u32[]{:S(2)}) %collective-permute-start.5) | collective-permute-done | bytes 3276832 | tf_op jit(solution)/shard_map/ppermute | solution.py:18
  1434.4 33.2 %fusion.11 = bf16[1280,1,2560]{2,0,1:T(8,128)(2,1)S(1)} fusion(s32[]{:T(128)S(6)} %select_n.129, bf16[160,2560]{1,0:T(8,128)(2,1)S(1)} %copy-done.14, bf16[160,2560]{1,0:T(8,128)(2,1)S(1)} %copy-done.18, bf16[320,2560]{1,0:T(8,128)(2,1)} %collective-permute-done.4, bf16[640,2560]{1,0:T(8,128)(2,1)S(1)} %collective-permute-done.5), kind=kLoop, calls=%fused_computation.34 | loop fusion | flops 52428800 | bytes 13107204 | tf_op jit(solution)/shard_map/stack | solution.py:260
  1476.6 43.6 %copy.65 = f32[1280,2,2560]{2,1,0:T(2,128)} copy(f32[1280,2,2560]{2,0,1:T(8,128)} %maximum_convert_fusion) | data formatting | bytes 52428800
  (364 shorter events, 261.5 us)
Async XLA Ops:
  11.8 52.9 %all-gather.10.cloned.1.call-start = ((), (), s32[]{:S(2)}) async-start(), calls=%async_computation.14 | async-start | bytes 1966080 | tf_op jit(solution)/shard_map/all_gather | solution.py:203
  12.6 63.5 %reduce-scatter.14.cloned.1.call-start = ((), (), s32[]{:S(2)}) async-start(), calls=%async_computation.11 | async-start | bytes 909312 | tf_op jit(solution)/shard_map/reduce_scatter | solution.py:163
  41.8 56.8 %reduce-scatter.12.cloned.1.call-start = ((), (), s32[]{:S(2)}) async-start(), calls=%async_computation.10 | async-start | bytes 15728640 | tf_op jit(solution)/shard_map/reduce_scatter | solution.py:157
  54.2 83.5 %reduce-scatter.18.cloned.1.call-start = ((), (), s32[]{:S(2)}) async-start(), calls=%async_computation.15 | async-start | bytes 7864320 | tf_op jit(solution)/shard_map/reduce_scatter | solution.py:205
  74.0 145.5 %all-gather.12.cloned.1.call-start = ((), (), s32[]{:S(2)}) async-start(), calls=%async_computation.16 | async-start | bytes 3932160 | tf_op jit(solution)/shard_map/all_gather | solution.py:222
  181.7 93.4 %reduce-scatter.28.cloned.1.call-start = ((), (), s32[]{:S(2)}) async-start(), calls=%async_computation.24 | async-start | bytes 1105920
  210.3 76.7 %all-gather.14.cloned.1.call-start = ((), (), s32[]{:S(2)}) async-start(), calls=%async_computation.17 | async-start | bytes 3932160 | tf_op jit(solution)/shard_map/all_gather | solution.py:229
  218.7 84.6 %all-gather.8.cloned.1.call-start = ((), (), s32[]{:S(2)}) async-start(), calls=%async_computation.12 | async-start | bytes 3932160 | tf_op jit(solution)/shard_map/all_gather | solution.py:194
  219.5 209.1 %reduce-scatter.22.cloned.1.call-start = ((), (), s32[]{:S(2)}) async-start(), calls=%async_computation.19 | async-start | bytes 7372800 | tf_op jit(solution)/shard_map/reduce_scatter | solution.py:71
  227.3 224.8 %all-reduce.30.cloned.1.call-start = ((), (), s32[]{:S(2)}) async-start(), calls=%async_computation.21 | async-start | bytes 262144 | tf_op jit(solution)/shard_map/psum | solution.py:74
  276.8 342.7 %all-reduce.32.cloned.1.call-start = ((), (), s32[]{:S(2)}) async-start(), calls=%async_computation.23 | async-start | bytes 327680 | tf_op jit(solution)/shard_map/psum | solution.py:277
  277.7 383.8 %reduce-scatter.20.cloned.1.call-start = ((), (), s32[]{:S(2)}) async-start(), calls=%async_computation.18 | async-start | bytes 3932160 | tf_op jit(solution)/shard_map/reduce_scatter | solution.py:231
  303.3 483.4 %reduce-scatter.26.cloned.1.call-start = ((), (), s32[]{:S(2)}) async-start(), calls=%async_computation.22 | async-start | bytes 7372800 | tf_op jit(solution)/shard_map/reduce_scatter | solution.py:71
  312.6 609.2 %reduce-scatter.24.cloned.1.call-start = ((), (), s32[]{:S(2)}) async-start(), calls=%async_computation.20 | async-start | bytes 7372800 | tf_op jit(solution)/shard_map/reduce_scatter | solution.py:71
  321.3 639.3 %reduce-scatter.16.cloned.1.call-start = ((), (), s32[]{:S(2)}) async-start(), calls=%async_computation.13 | async-start | bytes 3932160 | tf_op jit(solution)/shard_map/reduce_scatter | solution.py:196
  428.6 34.2 %collective-permute-start = (bf16[160,2560]{1,0:T(8,128)(2,1)}, bf16[160,2560]{1,0:T(8,128)(2,1)S(1)}, u32[]{:S(2)}, u32[]{:S(2)}) collective-permute-start(bf16[160,2560]{1,0:T(8,128)(2,1)} %reduce-scatter.22.cloned.1.call-done), channel_id=1, source_target_pairs={{0,28},{4,0},{8,4},{12,8},{16,12},{20,16},{24,20},{28,24},{1,29},{... | collective-permute-start | bytes 2457608 | tf_op jit(solution)/shard_map/ppermute | solution.py:18
  465.5 458.7 %collective-permute-start.1 = (bf16[320,2560]{1,0:T(8,128)(2,1)}, bf16[320,2560]{1,0:T(8,128)(2,1)}, u32[]{:S(2)}, u32[]{:S(2)}) collective-permute-start(bf16[320,2560]{1,0:T(8,128)(2,1)} %pad_maximum_fusion.3), channel_id=1, source_target_pairs={{0,24},{4,28},{8,0},{12,4},{16,8},{20,12},{24,16},{28,20},{1,25},{... | collective-permute-start | bytes 4915208 | tf_op jit(solution)/shard_map/ppermute | solution.py:18
  468.8 153.9 %collective-permute-start.8 = (bf16[640,296]{0,1:T(8,128)(2,1)S(1)}, bf16[640,296]{0,1:T(8,128)(2,1)S(1)}, u32[]{:S(2)}, u32[]{:S(2)}) collective-permute-start(bf16[640,296]{0,1:T(8,128)(2,1)S(1)} %pad_maximum_fusion.10), channel_id=1, source_target_pairs={{0,16},{4,20},{8,24},{12,28},{16,0},{20,4},{24,8},{28,12},{1,17},{... | collective-permute-start | bytes 1136648 | tf_op jit(solution)/shard_map/ppermute | solution.py:18
  786.7 141.4 %collective-permute-start.9 = (bf16[320,1280]{1,0:T(8,128)(2,1)}, bf16[320,1280]{1,0:T(8,128)(2,1)S(1)}, u32[]{:S(2)}, u32[]{:S(2)}) collective-permute-start(bf16[320,1280]{1,0:T(8,128)(2,1)} %reduce-scatter.26.cloned.1.call-done), channel_id=1, source_target_pairs={{0,28},{4,0},{8,4},{12,8},{16,12},{20,16},{24,20},{28,24},{1,29},{... | collective-permute-start | bytes 2457608 | tf_op jit(solution)/shard_map/ppermute | solution.py:18
  927.4 300.3 %collective-permute-start.2 = (bf16[640,2560]{1,0:T(8,128)(2,1)}, bf16[640,2560]{1,0:T(8,128)(2,1)}, u32[]{:S(2)}, u32[]{:S(2)}) collective-permute-start(bf16[640,2560]{1,0:T(8,128)(2,1)} %pad_maximum_fusion), channel_id=1, source_target_pairs={{0,16},{4,20},{8,24},{12,28},{16,0},{20,4},{24,8},{28,12},{1,17},{... | collective-permute-start | bytes 9830408 | tf_op jit(solution)/shard_map/ppermute | solution.py:18
  929.4 119.2 %collective-permute-start.10 = (bf16[640,1280]{1,0:T(8,128)(2,1)}, bf16[640,1280]{1,0:T(8,128)(2,1)S(1)}, u32[]{:S(2)}, u32[]{:S(2)}) collective-permute-start(bf16[640,1280]{1,0:T(8,128)(2,1)} %pad_maximum_fusion.5), channel_id=1, source_target_pairs={{0,24},{4,28},{8,0},{12,4},{16,8},{20,12},{24,16},{28,20},{1,25},{... | collective-permute-start | bytes 4915208 | tf_op jit(solution)/shard_map/ppermute | solution.py:18
  944.7 175.1 %collective-permute-start.4 = (bf16[320,2560]{1,0:T(8,128)(2,1)}, bf16[320,2560]{1,0:T(8,128)(2,1)}, u32[]{:S(2)}, u32[]{:S(2)}) collective-permute-start(bf16[320,2560]{1,0:T(8,128)(2,1)} %pad_maximum_fusion.4), channel_id=1, source_target_pairs={{0,24},{4,28},{8,0},{12,4},{16,8},{20,12},{24,16},{28,20},{1,25},{... | collective-permute-start | bytes 4915208 | tf_op jit(solution)/shard_map/ppermute | solution.py:18
  1048.9 471.3 %collective-permute-start.11 = (bf16[1280,1280]{1,0:T(8,128)(2,1)S(1)}, bf16[1280,1280]{1,0:T(8,128)(2,1)S(1)}, u32[]{:S(2)}, u32[]{:S(2)}) collective-permute-start(bf16[1280,1280]{1,0:T(8,128)(2,1)S(1)} %pad_maximum_fusion.2), channel_id=1, source_target_pairs={{0,16},{4,20},{8,24},{12,28},{16,0},{20,4},{24,8},{28,12},{1,17},{... | collective-permute-start | bytes 9830408 | tf_op jit(solution)/shard_map/ppermute | solution.py:18
  1121.4 313.1 %collective-permute-start.5 = (bf16[640,2560]{1,0:T(8,128)(2,1)S(1)}, bf16[640,2560]{1,0:T(8,128)(2,1)S(1)}, u32[]{:S(2)}, u32[]{:S(2)}) collective-permute-start(bf16[640,2560]{1,0:T(8,128)(2,1)S(1)} %pad_maximum_fusion.1), channel_id=1, source_target_pairs={{0,16},{4,20},{8,24},{12,28},{16,0},{20,4},{24,8},{28,12},{1,17},{... | collective-permute-start | bytes 9830408 | tf_op jit(solution)/shard_map/ppermute | solution.py:18
  (95 other events, 2561.4 us)
Sparse Core Ops, SparseCore 0:
  11.9 26.9 all-gather.5
  40.4 24.2 all-gather.9
  67.6 8.0 reduce-scatter.13
  78.4 20.1 reduce-scatter.11
  100.8 14.4 reduce-scatter.17
  181.8 12.5 all-gather.11
  210.4 64.6 reduce-scatter.27
  276.6 10.3 all-gather.13
  289.1 12.5 all-gather.7
  305.7 122.8 reduce-scatter.21
  431.5 20.5 all-reduce.29
  459.0 160.4 all-reduce.31
  621.9 39.5 reduce-scatter.19
  665.0 121.6 reduce-scatter.25
  791.1 130.6 reduce-scatter.23
  923.9 36.6 reduce-scatter.15
